TPU v7x, 32 devices: a whole 2x2x4 slice. The times are simulated.
32 devices in a mesh: grp: 2 (over y), row: 4 (over x, core), col: 4 (over z).
Axes of the slice: x: 2, y: 2, z: 4, core: 2. Of those that a mesh axis runs over, the one named last changes fastest.
Arguments:
- tokens: bfloat16 [256, 4096], P(('grp', 'row', 'col')), parts along dimension 0, may hold values from -6 to 6
- dec_bias: bfloat16 [4096], replicated, may hold values from -3 to 3
- enc_rows: bfloat16 [4096, 4096], P(None, ('row', 'col')), may hold values from -0.09375 to 0.09375
- bias_rows: bfloat16 [4096], P(('row', 'col')), may hold values from -3 to 3
- enc_cols: bfloat16 [4096, 16384], P(None, ('col', 'row')), may hold values from -0.09375 to 0.09375
- bias_cols: bfloat16 [16384], P(('col', 'row')), may hold values from -3 to 3
Outputs:
- slab: bfloat16 [8192, 16384], P(('grp', 'row'), 'col'), parts along dimension 0
There are 2 independent parts, one for each index of `grp`. A program takes and returns all parts, laid end to end along the dimension named above; an argument that names none is the same for every part. Nothing has to cross between parts.
All inputs are finite; a program needn't handle non-finite values.
Results may differ from a plain program's by a relative error of at most 0.0034.
Values may be sent and summed in bfloat16 or wider, within the bound.
A program may use at most 64 MiB of HBM per device.

v0:
```python
import jax
import jax.numpy as jnp
from jax import lax
from jax.sharding import PartitionSpec as P


def cross_codes(left, right):
    return lax.dot_general(
        left, right, (((0,), (0,)), ((), ())), preferred_element_type=jnp.float32
    )


def on_device(tokens, dec_bias, enc_rows, bias_rows, enc_cols, bias_cols):
    row_weight, row_bias = (enc_rows, bias_rows)
    row_width = row_weight.shape[1]
    joined_weight = jnp.concatenate([row_weight, enc_cols], axis=1)
    joined_bias = jnp.concatenate([row_bias, bias_cols], axis=0).astype(jnp.float32)
    shift_bias = dec_bias.astype(jnp.float32)
    centered = (
        lax.all_gather(tokens, ("row", "col"), axis=0, tiled=True).astype(jnp.float32) - shift_bias
    ).astype(jnp.bfloat16)
    pre_act = jnp.dot(centered, joined_weight, preferred_element_type=jnp.float32) + joined_bias
    codes = jax.nn.relu(pre_act).astype(jnp.bfloat16)
    total_tokens = codes.shape[0]
    row_own = codes[:, :row_width]
    col_own = codes[:, row_width:]
    col_full = lax.all_gather(col_own, "row", axis=1, tiled=True)
    summed = cross_codes(lax.all_gather(row_own, "col", axis=1, tiled=True), col_full)
    return (summed / total_tokens).astype(jnp.bfloat16)


def solution(mesh):
    in_specs = (
        P(("grp", "row", "col"), None),
        P(),
        P(None, ("row", "col")),
        P(("row", "col")),
        P(None, ("col", "row")),
        P(("col", "row")),
    )
    out_specs = P(("grp", "row"), "col")
    return jax.shard_map(
        on_device, mesh=mesh, in_specs=in_specs, out_specs=out_specs, check_vma=False
    )
```

profile of v0, /device:TPU:0, one launch (start us, length us, event | category | flops | bytes accessed | tf_op | source)
XLA Modules:
  0.0 86.5 jit_solution(15079428238558479330)
XLA Ops:
  6.5 0.0 all-gather.3.cloned.1.call-start
  6.5 0.7 all-gather.3.cloned.1.call-update
  7.3 0.0 all-gather.5.cloned.1.call-start
  7.3 0.7 convert_element_type.23
  8.0 0.7 maximum_convert_fusion
  8.7 41.6 %all-gather.3.cloned.1.call-done = bf16[128,4096]{1,0:T(8,128)(2,1)} async-done(((bf16[8,4096]{1,0:T(8,128)(2,1)}), bf16[128,4096]{1,0:T(8,128)(2,1)}) %all-gather.3.cloned.1.call-update) | async-done | bytes 1048592 | tf_op jit(solution)/shard_map/all_gather | solution.py:20
  50.3 5.9 %fusion.10 = bf16[128,1280]{1,0:T(8,128)(2,1)S(1)} fusion(bf16[4096,1024]{1,0:T(8,128)(2,1)} %param.10, bf16[4096,256]{1,0:T(8,128)(2,1)} %param.8, bf16[128,4096]{1,0:T(8,128)(2,1)} %all-gather.3.cloned.1.call-done, f32[4096]{0:T(1024)S(1)} %convert_element_type.23, f32[1280]{0:T(1024)S(1)} %maximum_convert_fusion), kind=kOutput, calls=%fused_computation.7 | convolution fusion | flops 1365213184 | bytes 11883520 | tf_op jit(solution)/shard_map/dot_general | solution.py:22
  56.1 0.7 slice.9
  56.9 0.0 all-gather.5.cloned.1.call-update
  56.9 13.8 %all_gather.10 = bf16[128,1024]{1,0:T(8,128)(2,1)S(1)} all-gather(bf16[128,256]{1,0:T(8,128)(2,1)S(1)} %slice.8), channel_id=1, replica_groups=mesh['grp'=2,'row'=4,'col'=4] {'col'}, dimensions={1}, use_global_device_ids=true | all-gather | bytes 327680 | tf_op jit(solution)/shard_map/all_gather | solution.py:28
  70.7 2.0 %all-gather.5.cloned.1.call-done = bf16[128,4096]{1,0:T(8,128)(2,1)} async-done(((bf16[128,1024]{1,0:T(8,128)(2,1)}), bf16[128,4096]{1,0:T(8,128)(2,1)}) %all-gather.5.cloned.1.call-update) | async-done | bytes 1048592 | tf_op jit(solution)/shard_map/all_gather | solution.py:27
  72.7 7.0 %multiply_convert_fusion = bf16[1024,4096]{1,0:T(8,128)(2,1)} fusion(bf16[128,1024]{1,0:T(8,128)(2,1)S(1)} %all_gather.10, bf16[128,4096]{1,0:T(8,128)(2,1)} %all-gather.5.cloned.1.call-done), kind=kOutput, calls=%fused_computation | convolution fusion | flops 1082130432 | bytes 9699328 | tf_op jit(solution)/shard_map/dot_general | solution.py:8
  (1 shorter events, 0.0 us)
Async XLA Ops:
  6.5 43.7 %all-gather.3.cloned.1.call-start = ((), (), s32[]{:S(2)}) async-start(), calls=%async_computation | async-start | bytes 1114112 | tf_op jit(solution)/shard_map/all_gather | solution.py:20
  7.3 65.4 %all-gather.5.cloned.1.call-start = ((), (), s32[]{:S(2)}) async-start(), calls=%async_computation.1 | async-start | bytes 1310720 | tf_op jit(solution)/shard_map/all_gather | solution.py:27
Sparse Core Ops, SparseCore 0:
  9.6 40.6 all-gather.2
  57.0 15.6 all-gather.4
where the time goes:
time: 86.8 us; the launch traced here: 86.5 us
  waiting for transfers between devices  44.3 us (51%)
  blocking collectives  13.8 us (16%)
  between operations  13.4 us (15%)
  matrix products  12.8 us (15%)
  other arithmetic  1.39 us (2%)
    all_gather x1, waiting for transfers between devices, on_device(): lax.all_gather(tokens, ('row', 'col'), axis=0, tiled=True)  41.6 us
    all_gather x1, blocking collectives, on_device(): lax.all_gather(row_own, 'col', axis=1, tiled=True)  13.8 us
    dot_general x1, matrix products, cross_codes(): lax.dot_general(left, right, (((0,), (0,)), ((), ())), preferred_element_...  6.99 us
    dot_general x1, matrix products, on_device(): jnp.dot(centered, joined_weight, preferred_element_type=jnp.float32)  5.85 us
    all_gather x1, waiting for transfers between devices, on_device(): col_full = lax.all_gather(col_own, 'row', axis=1, tiled=True)  1.99 us
  transfers between devices with their start and end apart: 2, of which 2 were waited for; matrix products, arithmetic and copies ran while one was open for 2% of the time, Pallas kernels for 0%

commit v1 on v0

v1 whole, which is shorter than its diff:
```python
import functools

import jax
import jax.numpy as jnp
from jax import lax
from jax.experimental import pallas as pl
from jax.experimental.pallas import tpu as pltpu
from jax.sharding import PartitionSpec as P

MESH = pl.DeviceIdType.MESH
CORES = 2
CHUNKS = 4
PIECE = 256


def gather_encode(
    n_row, n_col, tokens, dec_bias, enc_rows, bias_rows, enc_cols, bias_cols,
    rows_out, cols_out,
    tok, w_rows, w_cols, acc_rows, acc_cols, w_sem, own_sem,
    z_send, z_recv, x_send, x_recv, s_send, s_recv,
    rz_send, rz_recv, cx_send, cx_recv, cs_send, cs_recv,
):
    n_x = n_row // CORES
    r, c = lax.axis_index("row"), lax.axis_index("col")
    x, k = r // CORES, r % CORES
    other = 1 - k
    sibling = {"row": x * CORES + other, "col": c}
    block, width = tokens.shape
    part = width // CHUNKS
    n_piece, n_tok, piece = cols_out.shape[1:]

    def z_peer(s):
        return lax.rem(c + s, n_col)

    def x_peer(t):
        return {"row": lax.rem(x + t, n_x) * CORES + k, "col": c}

    def cols(d):
        return pl.ds(d * part, part)

    w_copies = []
    own_copies = []
    for d in range(CHUNKS):
        own = pltpu.make_async_copy(
            tokens.at[:, cols(d)], tok.at[k, x, c, :, cols(d)], own_sem.at[d]
        )
        own.start()
        own_copies.append(own)
    for d in range(CHUNKS):
        pair = (
            pltpu.make_async_copy(enc_rows.at[cols(d)], w_rows.at[cols(d)], w_sem.at[d, 0]),
            pltpu.make_async_copy(enc_cols.at[cols(d)], w_cols.at[cols(d)], w_sem.at[d, 1]),
        )
        for copy in pair:
            copy.start()
        w_copies.append(pair)

    barrier = pltpu.get_barrier_semaphore()
    for s in range(1, n_col):
        pl.semaphore_signal(barrier, inc=1, device_id={"row": r, "col": z_peer(s)}, device_id_type=MESH)
    for t in range(1, n_x):
        pl.semaphore_signal(barrier, inc=1, device_id=x_peer(t), device_id_type=MESH)
    pl.semaphore_signal(barrier, inc=1, device_id=sibling, device_id_type=MESH)
    pl.semaphore_wait(barrier, n_col - 1 + n_x - 1 + 1)

    def to_x(src, dst_c, d, s):
        for t in range(1, n_x):
            pltpu.make_async_remote_copy(
                src_ref=src, dst_ref=tok.at[k, x, dst_c, :, cols(d)],
                send_sem=x_send.at[d], recv_sem=x_recv.at[d, t, s],
                device_id=x_peer(t), device_id_type=MESH,
            ).start()

    def to_sibling(src, dst_x, dst_c, d):
        pltpu.make_async_remote_copy(
            src_ref=src, dst_ref=tok.at[k, dst_x, dst_c, :, cols(d)],
            send_sem=s_send.at[d], recv_sem=s_recv.at[d],
            device_id=sibling, device_id_type=MESH,
        ).start()

    for d in range(CHUNKS):
        src = tokens.at[:, cols(d)]
        for s in range(1, n_col):
            pltpu.make_async_remote_copy(
                src_ref=src, dst_ref=tok.at[k, x, c, :, cols(d)],
                send_sem=z_send.at[d], recv_sem=z_recv.at[d, s],
                device_id={"row": r, "col": z_peer(s)}, device_id_type=MESH,
            ).start()
        to_x(src, c, d, 0)
        to_sibling(src, x, c, d)

    def forward_z(d):
        for s in range(1, n_col):
            from_c = lax.rem(c + n_col - s, n_col)
            landed = tok.at[k, x, from_c, :, cols(d)]
            pltpu.make_async_copy(landed, landed, z_recv.at[d, s]).wait()
            to_x(landed, from_c, d, s)
            to_sibling(landed, x, from_c, d)

    def forward_x(d):
        for s in range(n_col):
            from_c = lax.rem(c + n_col - s, n_col)
            for t in range(1, n_x):
                from_x = lax.rem(x + n_x - t, n_x)
                landed = tok.at[k, from_x, from_c, :, cols(d)]
                pltpu.make_async_copy(landed, landed, x_recv.at[d, t, s]).wait()
                to_sibling(landed, from_x, from_c, d)

    def centered(d):
        landed = tok.at[other, :, :, :, cols(d)]
        pltpu.make_async_copy(landed, landed, s_recv.at[d]).wait()
        own_copies[d].wait()
        for copy in w_copies[d]:
            copy.wait()
        raw = tok[:, :, :, :, cols(d)].astype(jnp.float32).reshape(n_tok, part)
        return (raw - dec_bias[:, cols(d)].astype(jnp.float32)).astype(jnp.bfloat16)

    def dot(a, b):
        return jnp.dot(a, b, preferred_element_type=jnp.float32)

    forward_z(0)
    for d in range(CHUNKS):
        if d + 1 < CHUNKS:
            forward_z(d + 1)
        forward_x(d)
        cent = centered(d)
        if d + 1 < CHUNKS:
            new_rows = dot(cent, w_rows[cols(d)])
            acc_rows[...] = new_rows if d == 0 else acc_rows[...] + new_rows
            for p in range(n_piece):
                at = pl.ds(p * piece, piece)
                new = dot(cent, w_cols[cols(d), at])
                acc_cols[:, at] = new if d == 0 else acc_cols[:, at] + new

    last = CHUNKS - 1

    def finish(acc, weight, bias):
        total = dot(cent, weight)
        if last:
            total = total + acc
        return jax.nn.relu(total + bias.astype(jnp.float32)).astype(jnp.bfloat16)

    row_codes = finish(acc_rows[...], w_rows[cols(last)], bias_rows[...])
    rows_out[c] = row_codes.astype(jnp.float32).T.astype(jnp.bfloat16)
    row_copies = []
    for s in range(1, n_col):
        copy = pltpu.make_async_remote_copy(
            src_ref=rows_out.at[c], dst_ref=rows_out.at[c],
            send_sem=rz_send.at[s], recv_sem=rz_recv.at[s],
            device_id={"row": r, "col": z_peer(s)}, device_id_type=MESH,
        )
        copy.start()
        row_copies.append(copy)

    def codes_to_sibling(src_r, t, p):
        copy = pltpu.make_async_remote_copy(
            src_ref=cols_out.at[src_r, p], dst_ref=cols_out.at[src_r, p],
            send_sem=cs_send.at[t, p], recv_sem=cs_recv.at[t, p],
            device_id=sibling, device_id_type=MESH,
        )
        copy.start()
        return copy

    x_copies, s_copies = [], []
    for p in range(n_piece):
        at = pl.ds(p * piece, piece)
        cols_out[r, p] = finish(acc_cols[:, at], w_cols[cols(last), at], bias_cols[:, at])
        for t in range(1, n_x):
            copy = pltpu.make_async_remote_copy(
                src_ref=cols_out.at[r, p], dst_ref=cols_out.at[r, p],
                send_sem=cx_send.at[t, p], recv_sem=cx_recv.at[t, p],
                device_id=x_peer(t), device_id_type=MESH,
            )
            copy.start()
            x_copies.append(copy)
        s_copies.append(codes_to_sibling(r, 0, p))
    for p in range(n_piece):
        for t in range(1, n_x):
            from_r = lax.rem(x + n_x - t, n_x) * CORES + k
            landed = cols_out.at[from_r, p]
            pltpu.make_async_copy(landed, landed, cx_recv.at[t, p]).wait()
            s_copies.append(codes_to_sibling(from_r, t, p))

    for d in range(CHUNKS):
        some = tok.at[0, 0, pl.ds(0, n_col - 1), :, cols(d)]
        pltpu.make_async_copy(some, some, z_send.at[d]).wait()
        some = tok.at[0, pl.ds(0, n_x - 1), :, :, cols(d)]
        pltpu.make_async_copy(some, some, x_send.at[d]).wait()
        some = tok.at[0, :, :, :, cols(d)]
        pltpu.make_async_copy(some, some, s_send.at[d]).wait()
    for copy in row_copies:
        copy.wait()
    for copy in x_copies:
        copy.wait_send()
    for copy in s_copies:
        copy.wait()


def slab_kernel(scale, rows, cols, out):
    n_piece, _, piece = cols.shape[1:]
    left = rows[...].reshape(-1, rows.shape[2])
    for p in range(n_piece):
        total = jnp.dot(left, cols[0, p], preferred_element_type=jnp.float32)
        out[:, p * piece:(p + 1) * piece] = (total * scale).astype(jnp.bfloat16)


def on_device(n_row, n_col, tokens, dec_bias, enc_rows, bias_rows, enc_cols, bias_cols):
    block, width = tokens.shape
    n_tok = block * n_row * n_col
    n_x = n_row // CORES
    row_width, col_width = enc_rows.shape[1], enc_cols.shape[1]
    piece = min(PIECE, col_width)
    n_piece = col_width // piece
    dma = pltpu.SemaphoreType.DMA
    vmem = pl.BlockSpec(memory_space=pltpu.VMEM)
    anywhere = pl.BlockSpec(memory_space=pl.ANY)
    rows, cols = pl.pallas_call(
        functools.partial(gather_encode, n_row, n_col),
        out_shape=(
            jax.ShapeDtypeStruct((n_col, row_width, n_tok), jnp.bfloat16),
            jax.ShapeDtypeStruct((n_row, n_piece, n_tok, piece), jnp.bfloat16),
        ),
        in_specs=[anywhere, vmem, anywhere, vmem, anywhere, vmem],
        out_specs=(vmem, vmem),
        scratch_shapes=[
            pltpu.VMEM((CORES, n_x, n_col, block, width), jnp.bfloat16),
            pltpu.VMEM((width, row_width), jnp.bfloat16),
            pltpu.VMEM((width, col_width), jnp.bfloat16),
            pltpu.VMEM((n_tok, row_width), jnp.float32),
            pltpu.VMEM((n_tok, col_width), jnp.float32),
            dma((CHUNKS, 2)),
            dma((CHUNKS,)),
            dma((CHUNKS,)),
            dma((CHUNKS, n_col)),
            dma((CHUNKS,)),
            dma((CHUNKS, n_x, n_col)),
            dma((CHUNKS,)),
            dma((CHUNKS,)),
            dma((n_col,)),
            dma((n_col,)),
            dma((n_x, n_piece)),
            dma((n_x, n_piece)),
            dma((n_x, n_piece)),
            dma((n_x, n_piece)),
        ],
        compiler_params=pltpu.CompilerParams(
            collective_id=0, has_side_effects=True, vmem_limit_bytes=56 * 2**20
        ),
        name="gather_encode",
    )(
        tokens, dec_bias.reshape(1, -1), enc_rows, bias_rows.reshape(1, -1),
        enc_cols, bias_cols.reshape(1, -1),
    )
    return pl.pallas_call(
        functools.partial(slab_kernel, 1.0 / n_tok),
        out_shape=jax.ShapeDtypeStruct((n_col * row_width, n_row * col_width), jnp.bfloat16),
        grid=(n_row,),
        in_specs=[
            pl.BlockSpec((n_col, row_width, n_tok), lambda i: (0, 0, 0)),
            pl.BlockSpec((1, n_piece, n_tok, piece), lambda i: (i, 0, 0, 0)),
        ],
        out_specs=pl.BlockSpec((n_col * row_width, col_width), lambda i: (0, i)),
        compiler_params=pltpu.CompilerParams(vmem_limit_bytes=40 * 2**20),
        name="slab",
    )(rows, cols)


def solution(mesh):
    in_specs = (
        P(("grp", "row", "col"), None),
        P(),
        P(None, ("row", "col")),
        P(("row", "col")),
        P(None, ("col", "row")),
        P(("col", "row")),
    )
    out_specs = P(("grp", "row"), "col")
    return jax.shard_map(
        functools.partial(on_device, mesh.shape["row"], mesh.shape["col"]),
        mesh=mesh, in_specs=in_specs, out_specs=out_specs, check_vma=False,
    )
```

time: 86.8 us -> 42.7 us (0.49)
  waiting for transfers between devices: 44.3 us -> 0 us
  Pallas kernels: 0 us -> 36.4 us
  blocking collectives: 13.8 us -> 0 us
  between operations: 13.4 us -> 0.02 us
  matrix products: 12.8 us -> 0 us
  local copies, waits for them, and re-layouts: 0.74 us -> 5.99 us
  other arithmetic: 1.39 us -> 0 us
    all_gather x2 -> x0, waiting for transfers between devices: 43.6 us -> none  [the longest x1 41.6 us: on_device(): lax.all_gather(tokens, ('row', 'col'), axis=0, tiled=True)]
    pallas_call x0 -> x2, Pallas kernels: none -> 36.4 us  [the longest x1 31.7 us: on_device(): pl.pallas_call(functools.partial(gather_encode, n_row, n_col), out_shape=...]
    all_gather x1 -> x0, blocking collectives: 13.8 us -> none  [on_device(): lax.all_gather(row_own, 'col', axis=1, tiled=True)]
    dot_general x2 -> x0, matrix products: 12.8 us -> none  [the longest x1 6.99 us: cross_codes(): lax.dot_general(left, right, (((0,), (0,)), ((), ())), preferred_element_...]
    reshape x0 -> x3, local copies, waits for them, and re-layouts: none -> 3.82 us  [the longest x1 1.31 us: on_device(): dec_bias.reshape(1, -1)]
    unnamed x0 -> x4, local copies, waits for them, and re-layouts: none -> 2.17 us
    convert_element_type x2 -> x0, other arithmetic: 1.39 us -> none  [the longest x1 0.7 us: on_device(): shift_bias = dec_bias.astype(jnp.float32)]
  transfers between devices with their start and end apart: 2 -> 0, of which waited for: 2 -> 0; matrix products, arithmetic and copies ran while one was open for 2% -> 0% of each run, Pallas kernels for 0% -> 0%
where the time goes in v1:
time: 42.7 us; the launch traced here: 42.4 us
  Pallas kernels  36.4 us (85%)
  local copies, waits for them, and re-layouts  5.99 us (14%)
    pallas_call x1, Pallas kernels, on_device(): pl.pallas_call(functools.partial(gather_encode, n_row, n_col), out_shape=...  31.7 us
    pallas_call x1, Pallas kernels, on_device(): pl.pallas_call(functools.partial(slab_kernel, 1.0 / n_tok), out_shape=jax...  4.74 us
    unnamed x4, local copies, waits for them, and re-layouts  2.17 us
    reshape x1, local copies, waits for them, and re-layouts, on_device(): dec_bias.reshape(1, -1)  1.31 us
    reshape x1, local copies, waits for them, and re-layouts, on_device(): bias_cols.reshape(1, -1)  1.28 us
    reshape x1, local copies, waits for them, and re-layouts, on_device(): bias_rows.reshape(1, -1)  1.23 us

profile of v1, /device:TPU:0, one launch (start us, length us, event | category | flops | bytes accessed | tf_op | source)
XLA Modules:
  0.0 42.4 jit_solution(1882031824164683680)
XLA Ops:
  0.0 1.2 %reshape.10.bias_rows = bf16[1,256]{1,0:T(2,128)(2,1)} reshape(bf16[256]{0:T(256)(128)(2,1)} %param.9) | data formatting | bytes 1024 | tf_op jit(solution)/shard_map/reshape | solution.py:251
  1.2 1.3 %reshape.11.bias_cols = bf16[1,1024]{1,0:T(2,128)(2,1)} reshape(bf16[1024]{0:T(1024)(128)(2,1)} %param.11) | data formatting | bytes 4096 | tf_op jit(solution)/shard_map/reshape | solution.py:252
  2.5 1.3 %reshape.9.dec_bias = bf16[1,4096]{1,0:T(2,128)(2,1)} reshape(bf16[4096]{0:T(1024)(128)(2,1)} %param.7) | data formatting | bytes 16384 | tf_op jit(solution)/shard_map/reshape | solution.py:251
  3.8 31.7 %gather_encode.1 = (bf16[4,256,128]{2,1,0:T(8,128)(2,1)}, bf16[4,4,128,256]{3,2,1,0:T(8,128)(2,1)}) custom-call(bf16[8,4096]{1,0:T(8,128)(2,1)} %tokens.1, bf16[1,4096]{1,0:T(2,128)(2,1)} %reshape.9.dec_bias, bf16[4096,256]{1,0:T(8,128)(2,1)} %enc_rows.1, bf16[1,256]{1,0:T(2,128)(2,1)} %reshape.10.bias_rows, bf16[4096,1024]{1,0:T(8,128)(2,1)} %enc_cols.1, ...), custom_call_target="tpu_custom_call" | custom-call | tf_op jit(solution)/shard_map/gather_encode/pallas_call | solution.py:217
  35.5 0.0 copy-start
  35.5 1.2 %copy-done = bf16[4,4,128,256]{3,2,1,0:T(8,128)(2,1)S(1)} copy-done((bf16[4,4,128,256]{3,2,1,0:T(8,128)(2,1)S(1)}, bf16[4,4,128,256]{3,2,1,0:T(8,128)(2,1)}, u32[]{:S(2)}) %copy-start) | copy-done | bytes 1048600
  36.7 0.0 copy-start.1
  36.7 0.9 %copy-done.1 = bf16[4,256,128]{2,1,0:T(8,128)(2,1)S(1)} copy-done((bf16[4,256,128]{2,1,0:T(8,128)(2,1)S(1)}, bf16[4,256,128]{2,1,0:T(8,128)(2,1)}, u32[]{:S(2)}) %copy-start.1) | copy-done | bytes 262168
  37.7 4.7 %slab.1 = bf16[1024,4096]{1,0:T(8,128)(2,1)} custom-call(bf16[4,256,128]{2,1,0:T(8,128)(2,1)S(1)} %copy-done.1, bf16[4,4,128,256]{3,2,1,0:T(8,128)(2,1)S(1)} %copy-done), custom_call_target="tpu_custom_call" | custom-call | tf_op jit(solution)/shard_map/slab/pallas_call | solution.py:254
Async XLA Ops:
  35.5 1.2 %copy-start = (bf16[4,4,128,256]{3,2,1,0:T(8,128)(2,1)S(1)}, bf16[4,4,128,256]{3,2,1,0:T(8,128)(2,1)}, u32[]{:S(2)}) copy-start(bf16[4,4,128,256]{3,2,1,0:T(8,128)(2,1)} %get-tuple-element.8.cols) | copy-start | bytes 3145732
  36.7 0.9 %copy-start.1 = (bf16[4,256,128]{2,1,0:T(8,128)(2,1)S(1)}, bf16[4,256,128]{2,1,0:T(8,128)(2,1)}, u32[]{:S(2)}) copy-start(bf16[4,256,128]{2,1,0:T(8,128)(2,1)} %get-tuple-element.7.rows) | copy-start | bytes 786436

commit v2 on v0

v2 whole, which is shorter than its diff:
```python
import functools

import jax
import jax.numpy as jnp
from jax import lax
from jax.experimental import pallas as pl
from jax.experimental.pallas import tpu as pltpu
from jax.sharding import PartitionSpec as P

MESH = pl.DeviceIdType.MESH
CORES = 2
PIECE = 256


def gather_encode(
    n_row, n_col, tokens, dec_bias, enc_rows, bias_rows, enc_cols, bias_cols,
    rows_out, cols_out,
    tok, cent, w_rows, w_cols, shift, b_rows, b_cols, w_sem, b_sem, own_sem,
    z_send, z_recv, x_send, x_recv, s_send, s_recv,
    rz_send, rz_recv, cx_send, cx_recv, cs_send, cs_recv,
):
    n_x = n_row // CORES
    r, c = lax.axis_index("row"), lax.axis_index("col")
    x, k = r // CORES, r % CORES
    other = 1 - k
    sibling = {"row": x * CORES + other, "col": c}
    n_piece, n_tok, piece = cols_out.shape[1:]

    def z_peer(s):
        return {"row": r, "col": lax.rem(c + s, n_col)}

    def x_peer(t):
        return {"row": lax.rem(x + t, n_x) * CORES + k, "col": c}

    def from_c(s):
        return lax.rem(c + n_col - s, n_col)

    def from_x(t):
        return lax.rem(x + n_x - t, n_x)

    def local(src, dst, sem):
        copy = pltpu.make_async_copy(src, dst, sem)
        copy.start()
        return copy

    def remote(src, dst, send_sem, recv_sem, device):
        copy = pltpu.make_async_remote_copy(
            src_ref=src, dst_ref=dst, send_sem=send_sem, recv_sem=recv_sem,
            device_id=device, device_id_type=MESH,
        )
        copy.start()
        return copy

    def landed(ref, sem):
        pltpu.make_async_copy(ref, ref, sem).wait()

    barrier = pltpu.get_barrier_semaphore()
    for s in range(1, n_col):
        pl.semaphore_signal(barrier, inc=1, device_id=z_peer(s), device_id_type=MESH)
    for t in range(1, n_x):
        pl.semaphore_signal(barrier, inc=1, device_id=x_peer(t), device_id_type=MESH)
    pl.semaphore_signal(barrier, inc=1, device_id=sibling, device_id_type=MESH)

    own = local(tokens, tok.at[k, x, c], own_sem)
    b_copies = [
        local(dec_bias, shift, b_sem.at[0]),
        local(bias_rows, b_rows, b_sem.at[1]),
        local(bias_cols, b_cols, b_sem.at[2]),
    ]
    pl.semaphore_wait(barrier, n_col - 1 + n_x - 1 + 1)

    sent = []
    for s in range(1, n_col):
        sent.append(remote(tokens, tok.at[k, x, c], z_send.at[s], z_recv.at[s], z_peer(s)))
    for t in range(1, n_x):
        sent.append(remote(tokens, tok.at[k, x, c], x_send.at[t, 0], x_recv.at[t, 0], x_peer(t)))
    w_copies = [
        local(enc_cols, w_cols, w_sem.at[0]),
        local(enc_rows, w_rows, w_sem.at[1]),
    ]
    for s in range(1, n_col):
        block = tok.at[k, x, from_c(s)]
        landed(block, z_recv.at[s])
        for t in range(1, n_x):
            sent.append(remote(block, block, x_send.at[t, s], x_recv.at[t, s], x_peer(t)))
    own.wait()
    sent.append(remote(tok.at[k, x], tok.at[k, x], s_send.at[0], s_recv.at[0], sibling))
    for copy in b_copies:
        copy.wait()
    shift_row = shift[...].astype(jnp.float32).reshape(1, -1)

    def centre(kk, xx):
        raw = tok[kk, xx].astype(jnp.float32).reshape(cent.shape[2:])
        cent[kk, xx] = (raw - shift_row).astype(jnp.bfloat16)

    centre(k, x)
    for t in range(1, n_x):
        for s in range(n_col):
            landed(tok.at[k, from_x(t), from_c(s)], x_recv.at[t, s])
        plane = tok.at[k, from_x(t)]
        sent.append(remote(plane, plane, s_send.at[t], s_recv.at[t], sibling))
    for t in range(1, n_x):
        centre(k, from_x(t))
    for t in range(n_x):
        landed(tok.at[other, from_x(t)], s_recv.at[t])
        centre(other, from_x(t))

    def encode(weight, bias):
        total = jnp.dot(
            cent[...].reshape(n_tok, -1), weight, preferred_element_type=jnp.float32
        )
        return jax.nn.relu(total + bias).astype(jnp.bfloat16)

    row_bias = b_rows[...].astype(jnp.float32).reshape(1, -1)
    col_bias = b_cols[...].astype(jnp.float32).reshape(1, -1)
    w_copies[0].wait()
    for p in range(n_piece):
        at = slice(p * piece, (p + 1) * piece)
        cols_out[r, p] = encode(w_cols[:, at], col_bias[:, at])
        mine = cols_out.at[r, p]
        for t in range(1, n_x):
            sent.append(remote(mine, mine, cx_send.at[t, p], cx_recv.at[t, p], x_peer(t)))
        sent.append(remote(mine, mine, cs_send.at[0, p], cs_recv.at[0, p], sibling))
        if p == 0:
            w_copies[1].wait()
            rows_out[c] = encode(w_rows[...], row_bias).astype(jnp.float32).T.astype(jnp.bfloat16)
            for s in range(1, n_col):
                sent.append(
                    remote(rows_out.at[c], rows_out.at[c], rz_send.at[s], rz_recv.at[s], z_peer(s))
                )
    for p in range(n_piece):
        for t in range(1, n_x):
            theirs = cols_out.at[from_x(t) * CORES + k, p]
            landed(theirs, cx_recv.at[t, p])
            sent.append(remote(theirs, theirs, cs_send.at[t, p], cs_recv.at[t, p], sibling))

    for s in range(1, n_col):
        landed(rows_out.at[from_c(s)], rz_recv.at[s])
    for t in range(n_x):
        for p in range(n_piece):
            landed(cols_out.at[from_x(t) * CORES + other, p], cs_recv.at[t, p])
    for copy in sent:
        copy.wait_send()


def slab_kernel(scale, rows, cols, out):
    n_piece, _, piece = cols.shape[1:]
    left = rows[...].reshape(-1, rows.shape[2])
    for p in range(n_piece):
        total = jnp.dot(left, cols[0, p], preferred_element_type=jnp.float32)
        out[:, p * piece:(p + 1) * piece] = (total * scale).astype(jnp.bfloat16)


def on_device(n_row, n_col, tokens, dec_bias, enc_rows, bias_rows, enc_cols, bias_cols):
    block, width = tokens.shape
    n_tok = block * n_row * n_col
    n_x = n_row // CORES
    row_width, col_width = enc_rows.shape[1], enc_cols.shape[1]
    piece = min(PIECE, col_width)
    n_piece = col_width // piece
    dma = pltpu.SemaphoreType.DMA
    vmem = pl.BlockSpec(memory_space=pltpu.VMEM)
    anywhere = pl.BlockSpec(memory_space=pl.ANY)
    rows, cols = pl.pallas_call(
        functools.partial(gather_encode, n_row, n_col),
        out_shape=(
            pltpu.VMEM((n_col, row_width, n_tok), jnp.bfloat16),
            pltpu.VMEM((n_row, n_piece, n_tok, piece), jnp.bfloat16),
        ),
        in_specs=[anywhere] * 6,
        out_specs=(vmem, vmem),
        scratch_shapes=[
            pltpu.VMEM((CORES, n_x, n_col, block, width), jnp.bfloat16),
            pltpu.VMEM((CORES, n_x, n_col * block, width), jnp.bfloat16),
            pltpu.VMEM((width, row_width), jnp.bfloat16),
            pltpu.VMEM((width, col_width), jnp.bfloat16),
            pltpu.VMEM((width,), jnp.bfloat16),
            pltpu.VMEM((row_width,), jnp.bfloat16),
            pltpu.VMEM((col_width,), jnp.bfloat16),
            dma((2,)),
            dma((3,)),
            dma,
            dma((n_col,)),
            dma((n_col,)),
            dma((n_x, n_col)),
            dma((n_x, n_col)),
            dma((n_x,)),
            dma((n_x,)),
            dma((n_col,)),
            dma((n_col,)),
            dma((n_x, n_piece)),
            dma((n_x, n_piece)),
            dma((n_x, n_piece)),
            dma((n_x, n_piece)),
        ],
        compiler_params=pltpu.CompilerParams(
            collective_id=0, has_side_effects=True, vmem_limit_bytes=36 * 2**20
        ),
        name="gather_encode",
    )(
        tokens, dec_bias, enc_rows, bias_rows, enc_cols, bias_cols
    )
    return pl.pallas_call(
        functools.partial(slab_kernel, 1.0 / n_tok),
        out_shape=jax.ShapeDtypeStruct((n_col * row_width, n_row * col_width), jnp.bfloat16),
        grid=(n_row,),
        in_specs=[
            pl.BlockSpec((n_col, row_width, n_tok), lambda i: (0, 0, 0)),
            pl.BlockSpec((1, n_piece, n_tok, piece), lambda i: (i, 0, 0, 0)),
        ],
        out_specs=pl.BlockSpec((n_col * row_width, col_width), lambda i: (0, i)),
        compiler_params=pltpu.CompilerParams(vmem_limit_bytes=40 * 2**20),
        name="slab",
    )(rows, cols)


def solution(mesh):
    in_specs = (
        P(("grp", "row", "col"), None),
        P(),
        P(None, ("row", "col")),
        P(("row", "col")),
        P(None, ("col", "row")),
        P(("col", "row")),
    )
    out_specs = P(("grp", "row"), "col")
    return jax.shard_map(
        functools.partial(on_device, mesh.shape["row"], mesh.shape["col"]),
        mesh=mesh, in_specs=in_specs, out_specs=out_specs, check_vma=False,
    )
```

time: 86.8 us -> 37.9 us (0.44)
  waiting for transfers between devices: 44.3 us -> 0 us
  Pallas kernels: 0 us -> 29.8 us
  blocking collectives: 13.8 us -> 0 us
  between operations: 13.4 us -> 0.02 us
  matrix products: 12.8 us -> 0 us
  local copies, waits for them, and re-layouts: 0.74 us -> 7.84 us
  other arithmetic: 1.39 us -> 0 us
    all_gather x2 -> x0, waiting for transfers between devices: 43.6 us -> none  [the longest x1 41.6 us: on_device(): lax.all_gather(tokens, ('row', 'col'), axis=0, tiled=True)]
    pallas_call x0 -> x2, Pallas kernels: none -> 29.8 us  [the longest x1 25 us: on_device(): pl.pallas_call(functools.partial(gather_encode, n_row, n_col), out_shape=...]
    all_gather x1 -> x0, blocking collectives: 13.8 us -> none  [on_device(): lax.all_gather(row_own, 'col', axis=1, tiled=True)]
    dot_general x2 -> x0, matrix products: 12.8 us -> none  [the longest x1 6.99 us: cross_codes(): lax.dot_general(left, right, (((0,), (0,)), ((), ())), preferred_element_...]
    unnamed x0 -> x12, local copies, waits for them, and re-layouts: none -> 7.84 us
    convert_element_type x2 -> x0, other arithmetic: 1.39 us -> none  [the longest x1 0.7 us: on_device(): shift_bias = dec_bias.astype(jnp.float32)]
  transfers between devices with their start and end apart: 2 -> 0, of which waited for: 2 -> 0; matrix products, arithmetic and copies ran while one was open for 2% -> 0% of each run, Pallas kernels for 0% -> 0%
where the time goes in v2:
time: 37.9 us; the launch traced here: 37.6 us
  Pallas kernels  29.8 us (79%)
  local copies, waits for them, and re-layouts  7.84 us (21%)
    pallas_call x1, Pallas kernels, on_device(): pl.pallas_call(functools.partial(gather_encode, n_row, n_col), out_shape=...  25 us
    unnamed x12, local copies, waits for them, and re-layouts  7.84 us
    pallas_call x1, Pallas kernels, on_device(): pl.pallas_call(functools.partial(slab_kernel, 1.0 / n_tok), out_shape=jax...  4.77 us

profile of v2, /device:TPU:0, one launch (start us, length us, event | category | flops | bytes accessed | tf_op | source)
XLA Modules:
  0.0 37.6 jit_solution(18270822645022597323)
XLA Ops:
  0.0 0.0 copy-start
  0.0 3.4 %copy-done = bf16[4096,1024]{1,0:T(8,128)(2,1)S(1)} copy-done((bf16[4096,1024]{1,0:T(8,128)(2,1)S(1)}, bf16[4096,1024]{1,0:T(8,128)(2,1)}, u32[]{:S(2)}) %copy-start) | copy-done | bytes 8388632
  3.4 0.0 copy-start.1
  3.4 1.6 %copy-done.1 = bf16[4096,256]{1,0:T(8,128)(2,1)S(1)} copy-done((bf16[4096,256]{1,0:T(8,128)(2,1)S(1)}, bf16[4096,256]{1,0:T(8,128)(2,1)}, u32[]{:S(2)}) %copy-start.1) | copy-done | bytes 2097176
  5.0 0.0 copy-start.2
  5.0 0.8 %copy-done.2 = bf16[8,4096]{1,0:T(8,128)(2,1)S(1)} copy-done((bf16[8,4096]{1,0:T(8,128)(2,1)S(1)}, bf16[8,4096]{1,0:T(8,128)(2,1)}, u32[]{:S(2)}) %copy-start.2) | copy-done | bytes 65560
  5.8 0.0 copy-start.3
  5.8 0.7 %copy-done.3 = bf16[4096]{0:T(1024)(128)(2,1)S(1)} copy-done((bf16[4096]{0:T(1024)(128)(2,1)S(1)}, bf16[4096]{0:T(1024)(128)(2,1)}, u32[]{:S(2)}) %copy-start.3) | copy-done | bytes 8216
  6.5 0.0 copy-start.4
  6.5 0.7 %copy-done.4 = bf16[1024]{0:T(1024)(128)(2,1)S(1)} copy-done((bf16[1024]{0:T(1024)(128)(2,1)S(1)}, bf16[1024]{0:T(1024)(128)(2,1)}, u32[]{:S(2)}) %copy-start.4) | copy-done | bytes 2072
  7.2 0.0 copy-start.5
  7.2 0.7 %copy-done.5 = bf16[256]{0:T(256)(128)(2,1)S(1)} copy-done((bf16[256]{0:T(256)(128)(2,1)S(1)}, bf16[256]{0:T(256)(128)(2,1)}, u32[]{:S(2)}) %copy-start.5) | copy-done | bytes 536
  7.8 25.0 %gather_encode.1 = (bf16[4,256,128]{2,1,0:T(8,128)(2,1)S(1)}, bf16[4,4,128,256]{3,2,1,0:T(8,128)(2,1)S(1)}) custom-call(bf16[8,4096]{1,0:T(8,128)(2,1)S(1)} %copy-done.2, bf16[4096]{0:T(1024)(128)(2,1)S(1)} %copy-done.3, bf16[4096,256]{1,0:T(8,128)(2,1)S(1)} %copy-done.1, bf16[256]{0:T(256)(128)(2,1)S(1)} %copy-done.5, bf16[4096,1024]{1,0:T(8,128)(2,1)S(1)} %copy-done, ...), custom_call_target="tpu_custom_call" | custom-call | tf_op jit(solution)/shard_map/gather_encode/pallas_call | solution.py:164
  32.9 4.8 %slab.1 = bf16[1024,4096]{1,0:T(8,128)(2,1)} custom-call(bf16[4,256,128]{2,1,0:T(8,128)(2,1)S(1)} %get-tuple-element.7.rows, bf16[4,4,128,256]{3,2,1,0:T(8,128)(2,1)S(1)} %get-tuple-element.8.cols), custom_call_target="tpu_custom_call" | custom-call | tf_op jit(solution)/shard_map/slab/pallas_call | solution.py:203
Async XLA Ops:
  0.0 3.4 %copy-start = (bf16[4096,1024]{1,0:T(8,128)(2,1)S(1)}, bf16[4096,1024]{1,0:T(8,128)(2,1)}, u32[]{:S(2)}) copy-start(bf16[4096,1024]{1,0:T(8,128)(2,1)} %enc_cols.1) | copy-start | bytes 25165828
  3.4 1.6 %copy-start.1 = (bf16[4096,256]{1,0:T(8,128)(2,1)S(1)}, bf16[4096,256]{1,0:T(8,128)(2,1)}, u32[]{:S(2)}) copy-start(bf16[4096,256]{1,0:T(8,128)(2,1)} %enc_rows.1) | copy-start | bytes 6291460
  5.0 0.8 %copy-start.2 = (bf16[8,4096]{1,0:T(8,128)(2,1)S(1)}, bf16[8,4096]{1,0:T(8,128)(2,1)}, u32[]{:S(2)}) copy-start(bf16[8,4096]{1,0:T(8,128)(2,1)} %tokens.1) | copy-start | bytes 196612
  5.8 0.7 %copy-start.3 = (bf16[4096]{0:T(1024)(128)(2,1)S(1)}, bf16[4096]{0:T(1024)(128)(2,1)}, u32[]{:S(2)}) copy-start(bf16[4096]{0:T(1024)(128)(2,1)} %dec_bias.1) | copy-start | bytes 24580
  6.5 0.7 %copy-start.4 = (bf16[1024]{0:T(1024)(128)(2,1)S(1)}, bf16[1024]{0:T(1024)(128)(2,1)}, u32[]{:S(2)}) copy-start(bf16[1024]{0:T(1024)(128)(2,1)} %bias_cols.1) | copy-start | bytes 6148
  7.2 0.7 %copy-start.5 = (bf16[256]{0:T(256)(128)(2,1)S(1)}, bf16[256]{0:T(256)(128)(2,1)}, u32[]{:S(2)}) copy-start(bf16[256]{0:T(256)(128)(2,1)} %bias_rows.1) | copy-start | bytes 1540

commit v3 on v2

--- a/solution.py
+++ b/solution.py
@@ -67,17 +67,17 @@
         local(bias_rows, b_rows, b_sem.at[1]),
         local(bias_cols, b_cols, b_sem.at[2]),
     ]
-    pl.semaphore_wait(barrier, n_col - 1 + n_x - 1 + 1)
-
-    sent = []
-    for s in range(1, n_col):
-        sent.append(remote(tokens, tok.at[k, x, c], z_send.at[s], z_recv.at[s], z_peer(s)))
-    for t in range(1, n_x):
-        sent.append(remote(tokens, tok.at[k, x, c], x_send.at[t, 0], x_recv.at[t, 0], x_peer(t)))
     w_copies = [
         local(enc_cols, w_cols, w_sem.at[0]),
         local(enc_rows, w_rows, w_sem.at[1]),
     ]
+    pl.semaphore_wait(barrier, n_col - 1 + n_x - 1 + 1)
+
+    sent = []
+    for s in range(1, n_col):
+        sent.append(remote(tokens, tok.at[k, x, c], z_send.at[s], z_recv.at[s], z_peer(s)))
+    for t in range(1, n_x):
+        sent.append(remote(tokens, tok.at[k, x, c], x_send.at[t, 0], x_recv.at[t, 0], x_peer(t)))
     for s in range(1, n_col):
         block = tok.at[k, x, from_c(s)]
         landed(block, z_recv.at[s])
@@ -143,12 +143,25 @@
         copy.wait_send()
 
 
-def slab_kernel(scale, rows, cols, out):
-    n_piece, _, piece = cols.shape[1:]
+def slab_kernel(scale, rows, cols, out, held, sem):
+    n_row, n_piece, _, piece = cols.shape
     left = rows[...].reshape(-1, rows.shape[2])
-    for p in range(n_piece):
-        total = jnp.dot(left, cols[0, p], preferred_element_type=jnp.float32)
-        out[:, p * piece:(p + 1) * piece] = (total * scale).astype(jnp.bfloat16)
+
+    def copy(i, p):
+        at = pl.ds(pl.multiple_of((i * n_piece + p) * piece, piece), piece)
+        return pltpu.make_async_copy(held.at[i, p], out.at[:, at], sem.at[i, p])
+
+    @pl.loop(0, n_row)
+    def _(i):
+        for p in range(n_piece):
+            total = jnp.dot(left, cols[i, p], preferred_element_type=jnp.float32)
+            held[i, p] = (total * scale).astype(jnp.bfloat16)
+            copy(i, p).start()
+
+    @pl.loop(0, n_row)
+    def _(i):
+        for p in range(n_piece):
+            copy(i, p).wait()
 
 
 def on_device(n_row, n_col, tokens, dec_bias, enc_rows, bias_rows, enc_cols, bias_cols):
@@ -158,9 +171,10 @@
     row_width, col_width = enc_rows.shape[1], enc_cols.shape[1]
     piece = min(PIECE, col_width)
     n_piece = col_width // piece
+    out_bytes = 2 * n_tok * (n_col * row_width + n_row * col_width)
     dma = pltpu.SemaphoreType.DMA
     vmem = pl.BlockSpec(memory_space=pltpu.VMEM)
-    anywhere = pl.BlockSpec(memory_space=pl.ANY)
+    anywhere = pl.BlockSpec(memory_space=pltpu.HBM)
     rows, cols = pl.pallas_call(
         functools.partial(gather_encode, n_row, n_col),
         out_shape=(
@@ -194,7 +208,7 @@
             dma((n_x, n_piece)),
         ],
         compiler_params=pltpu.CompilerParams(
-            collective_id=0, has_side_effects=True, vmem_limit_bytes=36 * 2**20
+            collective_id=0, has_side_effects=True, vmem_limit_bytes=57 * 2**20 - out_bytes
         ),
         name="gather_encode",
     )(
@@ -203,12 +217,12 @@
     return pl.pallas_call(
         functools.partial(slab_kernel, 1.0 / n_tok),
         out_shape=jax.ShapeDtypeStruct((n_col * row_width, n_row * col_width), jnp.bfloat16),
-        grid=(n_row,),
-        in_specs=[
-            pl.BlockSpec((n_col, row_width, n_tok), lambda i: (0, 0, 0)),
-            pl.BlockSpec((1, n_piece, n_tok, piece), lambda i: (i, 0, 0, 0)),
+        in_specs=[vmem, vmem],
+        out_specs=anywhere,
+        scratch_shapes=[
+            pltpu.VMEM((n_row, n_piece, n_col * row_width, piece), jnp.bfloat16),
+            dma((n_row, n_piece)),
         ],
-        out_specs=pl.BlockSpec((n_col * row_width, col_width), lambda i: (0, i)),
         compiler_params=pltpu.CompilerParams(vmem_limit_bytes=40 * 2**20),
         name="slab",
     )(rows, cols)

time: 37.9 us -> 29.7 us (0.78)
  local copies, waits for them, and re-layouts: 7.84 us -> 0 us
    unnamed x12 -> x0, local copies, waits for them, and re-layouts: 7.84 us -> none
    pallas_call x1, Pallas kernels: 4.77 us -> 4.28 us  [on_device(): pl.pallas_call(functools.partial(slab_kernel, 1.0 / n_tok), out_shape=jax...]
where the time goes in v3:
time: 29.7 us; the launch traced here: 29.5 us
  Pallas kernels  29.5 us (99%)
    pallas_call x1, Pallas kernels, on_device(): pl.pallas_call(functools.partial(gather_encode, n_row, n_col), out_shape=...  25.2 us
    pallas_call x1, Pallas kernels, on_device(): pl.pallas_call(functools.partial(slab_kernel, 1.0 / n_tok), out_shape=jax...  4.28 us

profile of v3, /device:TPU:0, one launch (start us, length us, event | category | flops | bytes accessed | tf_op | source)
XLA Modules:
  0.0 29.5 jit_solution(6798850799549262241)
XLA Ops:
  0.0 25.2 %gather_encode.1 = (bf16[4,256,128]{2,1,0:T(8,128)(2,1)S(1)}, bf16[4,4,128,256]{3,2,1,0:T(8,128)(2,1)S(1)}) custom-call(bf16[8,4096]{1,0:T(8,128)(2,1)} %tokens.1, bf16[4096]{0:T(1024)(128)(2,1)} %dec_bias.1, bf16[4096,256]{1,0:T(8,128)(2,1)} %enc_rows.1, bf16[256]{0:T(256)(128)(2,1)} %bias_rows.1, bf16[4096,1024]{1,0:T(8,128)(2,1)} %enc_cols.1, ...), custom_call_target="tpu_custom_call" | custom-call | tf_op jit(solution)/shard_map/gather_encode/pallas_call | solution.py:178
  25.3 4.3 %slab.1 = bf16[1024,4096]{1,0:T(8,128)(2,1)} custom-call(bf16[4,256,128]{2,1,0:T(8,128)(2,1)S(1)} %get-tuple-element.7.rows, bf16[4,4,128,256]{3,2,1,0:T(8,128)(2,1)S(1)} %get-tuple-element.8.cols), custom_call_target="tpu_custom_call" | custom-call | tf_op jit(solution)/shard_map/slab/pallas_call | solution.py:217

commit v4 on v3

--- a/solution.py
+++ b/solution.py
@@ -144,24 +144,25 @@
 
 
 def slab_kernel(scale, rows, cols, out, held, sem):
+    n_col, row_width, _ = rows.shape
     n_row, n_piece, _, piece = cols.shape
-    left = rows[...].reshape(-1, rows.shape[2])
-
-    def copy(i, p):
-        at = pl.ds(pl.multiple_of((i * n_piece + p) * piece, piece), piece)
-        return pltpu.make_async_copy(held.at[i, p], out.at[:, at], sem.at[i, p])
-
-    @pl.loop(0, n_row)
-    def _(i):
-        for p in range(n_piece):
-            total = jnp.dot(left, cols[i, p], preferred_element_type=jnp.float32)
-            held[i, p] = (total * scale).astype(jnp.bfloat16)
-            copy(i, p).start()
-
-    @pl.loop(0, n_row)
-    def _(i):
-        for p in range(n_piece):
-            copy(i, p).wait()
+
+    def copy(b):
+        at = pl.ds(pl.multiple_of(b * row_width, row_width), row_width)
+        return pltpu.make_async_copy(held.at[b], out.at[at], sem.at[b])
+
+    @pl.loop(0, n_col)
+    def _(b):
+        for i in range(n_row):
+            for p in range(n_piece):
+                first = (i * n_piece + p) * piece
+                total = jnp.dot(rows[b], cols[i, p], preferred_element_type=jnp.float32)
+                held[b, :, first:first + piece] = (total * scale).astype(jnp.bfloat16)
+        copy(b).start()
+
+    @pl.loop(0, n_col)
+    def _(b):
+        copy(b).wait()
 
 
 def on_device(n_row, n_col, tokens, dec_bias, enc_rows, bias_rows, enc_cols, bias_cols):
@@ -220,8 +221,8 @@
         in_specs=[vmem, vmem],
         out_specs=anywhere,
         scratch_shapes=[
-            pltpu.VMEM((n_row, n_piece, n_col * row_width, piece), jnp.bfloat16),
-            dma((n_row, n_piece)),
+            pltpu.VMEM((n_col, row_width, n_row * col_width), jnp.bfloat16),
+            dma((n_col,)),
         ],
         compiler_params=pltpu.CompilerParams(vmem_limit_bytes=40 * 2**20),
         name="slab",

time: 29.7 us -> 29.5 us (level)
  no operation moved by 1% of the time
where the time goes in v4:
time: 29.5 us; the launch traced here: 29.4 us
  Pallas kernels  29.4 us (100%)
    pallas_call x1, Pallas kernels, on_device(): pl.pallas_call(functools.partial(gather_encode, n_row, n_col), out_shape=...  25.2 us
    pallas_call x1, Pallas kernels, on_device(): pl.pallas_call(functools.partial(slab_kernel, 1.0 / n_tok), out_shape=jax...  4.12 us

profile of v4, /device:TPU:0, one launch (start us, length us, event | category | flops | bytes accessed | tf_op | source)
XLA Modules:
  0.0 29.4 jit_solution(17192838257888864316)
XLA Ops:
  0.0 25.2 %gather_encode.1 = (bf16[4,256,128]{2,1,0:T(8,128)(2,1)S(1)}, bf16[4,4,128,256]{3,2,1,0:T(8,128)(2,1)S(1)}) custom-call(bf16[8,4096]{1,0:T(8,128)(2,1)} %tokens.1, bf16[4096]{0:T(1024)(128)(2,1)} %dec_bias.1, bf16[4096,256]{1,0:T(8,128)(2,1)} %enc_rows.1, bf16[256]{0:T(256)(128)(2,1)} %bias_rows.1, bf16[4096,1024]{1,0:T(8,128)(2,1)} %enc_cols.1, ...), custom_call_target="tpu_custom_call" | custom-call | tf_op jit(solution)/shard_map/gather_encode/pallas_call | solution.py:179
  25.3 4.1 %slab.1 = bf16[1024,4096]{1,0:T(8,128)(2,1)} custom-call(bf16[4,256,128]{2,1,0:T(8,128)(2,1)S(1)} %get-tuple-element.7.rows, bf16[4,4,128,256]{3,2,1,0:T(8,128)(2,1)S(1)} %get-tuple-element.8.cols), custom_call_target="tpu_custom_call" | custom-call | tf_op jit(solution)/shard_map/slab/pallas_call | solution.py:218
